TPU v7x, 32 devices: a whole 2x2x4 slice. The times are simulated.
32 devices in a mesh: pairs: 8 (over z, y), coup: 4 (over x, core).
Axes of the slice: x: 2, y: 2, z: 4, core: 2. Of those that a mesh axis runs over, the one named last changes fastest.
Arguments:
- coupling_list: int32 [3, 128], P(None, 'pairs'), may hold values from 0 to 127, as said below
- pair_slot: int32 [32], replicated, may hold values from 0 to 31, as said below
- coupling_weight: float32 [128], P('pairs'), may hold values from -1 to 1
- integrals: bfloat16 [32, 448, 448], P(('pairs', 'coup')), may hold values from -6 to 6
- orbital_energy: float32 [32, 448], P(('pairs', 'coup')), may hold values from 0.5 to 3
- pair_energy: float32 [32], P(('pairs', 'coup')), may hold values from 0.3 to 3
- intersections: bfloat16 [128, 448, 448], P(('pairs', 'coup')), may hold values from -0.25 to 0.25
Outputs:
- amplitudes: float32 [32, 448, 448], P(('pairs', 'coup'))
Inputs may be any that keep to these rules, and one draw needn't show every extreme that they name: `coupling_list`: row 0 and row 1 hold pair numbers, row 2 an intersection index. Positions g * 16 to (g + 1) * 16 - 1 form block g: its pairs i have rows (pair_slot) in g * 4 to (g + 1) * 4 - 1 and its intersection indices lie in g * 16 to (g + 1) * 16 - 1; for every h, exactly two couplings of block g have pair j with its row in h * 4 to (h + 1) * 4 - 1, and both name the same pair j. In each block at most 8 couplings have pair i with its row in the same 1 row of one device, and exactly 8 do for one such device. Likewise in each block at most 8 couplings have an intersection index among the same 4 indices of one device, and exactly 8 do for one such device. `pair_slot`: A permutation of the pairs.
All inputs are finite; a program needn't handle non-finite values.
Results may differ from a plain program's by a relative error of at most 0.0024.
Values may be sent and summed in bfloat16 or wider, within the bound.
A program may use at most 128 MiB of HBM per device.

v0:
```python
import math

import jax
import jax.numpy as jnp
from jax import lax
from jax.sharding import PartitionSpec as P

ITERS = 2


def lookup(lookup_table, queries):
    columns = lax.broadcasted_iota(jnp.int32, (queries.shape[0], lookup_table.shape[0]), 1)
    return jnp.sum(jnp.where(queries[:, None] == columns, lookup_table[None, :], 0), axis=1)


def compact(chosen, slot_count):
    order_rank = jnp.cumsum(chosen.astype(jnp.int32)) - 1
    target = lax.broadcasted_iota(jnp.int32, (slot_count, chosen.shape[0]), 0)
    return chosen[None, :] & (order_rank[None, :] == target)


def pick_values(selected, values):
    return jnp.sum(jnp.where(selected, values[None, :], jnp.zeros((), values.dtype)), axis=1)


def per_device(
    coupling_list, pair_slot, coupling_weight, integrals, orbital_energy, pair_energy, intersections
):
    group_total = lax.axis_size("pairs")
    coup_total = lax.axis_size("coup")
    group_index = lax.axis_index("pairs")
    member = lax.axis_index("coup")
    pair_dev = integrals.shape[0]
    ov_dev = intersections.shape[0]
    feature_width = integrals.shape[-1]
    group_pairs = pair_dev * coup_total
    group_couplings = coupling_list.shape[1]
    group_intersections = ov_dev * coup_total
    owner_row = lookup(pair_slot, coupling_list[0])
    reader_row = lookup(pair_slot, coupling_list[1])
    local_pair = owner_row - group_index * group_pairs
    source = reader_row // group_pairs
    read_pair = reader_row % group_pairs
    local_intersection = coupling_list[2] - group_index * group_intersections
    ovl_table = lax.all_gather(intersections, "coup", axis=0, tiled=True)
    slot_count = group_couplings // 2
    assigned = local_pair // pair_dev == member
    row_offset = member * pair_dev
    intersection_offset = 0
    selected = compact(assigned, slot_count)
    slot_source = pick_values(selected, source)
    slot_intersection = jnp.maximum(
        pick_values(selected, local_intersection) - intersection_offset, 0
    )
    slot_pair = pick_values(selected, local_pair) - row_offset
    slot_weight = pick_values(selected, coupling_weight)
    sources = lax.broadcasted_iota(jnp.int32, (group_total, group_couplings), 0)
    asked_for = source[None, :] == sources
    wanted_here = jnp.max(jnp.where(asked_for, read_pair[None, :], -1), axis=1)
    wanted = lax.all_to_all(wanted_here, "pairs", split_axis=0, concat_axis=0, tiled=True)
    denominator = (
        orbital_energy[:, :, None] + orbital_energy[:, None, :] + pair_energy[:, None, None]
    )
    integral_f = integrals.astype(jnp.float32)
    amplitudes = -integral_f / denominator
    block_size = math.gcd(slot_count, 8)
    for iteration in range(ITERS):
        rounded = amplitudes.astype(jnp.bfloat16)
        strips = lax.all_to_all(rounded, "coup", split_axis=1, concat_axis=0, tiled=True)
        outgoing = jnp.take(strips, wanted, axis=0)
        arrived = lax.all_to_all(outgoing, "pairs", split_axis=0, concat_axis=0, tiled=True)
        fetched = lax.all_gather(arrived, "coup", axis=1, tiled=True)

        def accumulate(block_turn, partial_value):
            first_slot = block_turn * block_size
            source_block = lax.dynamic_slice_in_dim(slot_source, first_slot, block_size)
            intersection_block = lax.dynamic_slice_in_dim(slot_intersection, first_slot, block_size)
            pair_block = lax.dynamic_slice_in_dim(slot_pair, first_slot, block_size)
            weight_block = lax.dynamic_slice_in_dim(slot_weight, first_slot, block_size)
            amp_block = jnp.take(fetched, source_block, axis=0)
            ovl_block = jnp.take(ovl_table, intersection_block, axis=0)
            left_product = jnp.einsum(
                "sab,sbc->sac", ovl_block, amp_block, preferred_element_type=jnp.float32
            ).astype(jnp.bfloat16)
            full_product = jnp.einsum(
                "sac,sdc->sad", left_product, ovl_block, preferred_element_type=jnp.float32
            )
            row_index = lax.broadcasted_iota(jnp.int32, (pair_dev, block_size), 0)
            spread = jnp.where(pair_block[None, :] == row_index, weight_block[None, :], 0.0)
            return partial_value + jnp.einsum(
                "ps,sad->pad", spread, full_product, precision=lax.Precision.HIGHEST
            )

        partial_value = lax.fori_loop(
            0,
            slot_count // block_size,
            accumulate,
            jnp.zeros((pair_dev, feature_width, feature_width), jnp.float32),
        )
        amplitudes = -(integral_f + partial_value) / denominator
    return amplitudes


def solution(mesh):
    in_specs = (
        P(None, "pairs"),
        P(),
        P("pairs"),
        P(("pairs", "coup"), None, None),
        P(("pairs", "coup"), None),
        P(("pairs", "coup")),
        P(("pairs", "coup"), None, None),
    )
    out_specs = P(("pairs", "coup"), None, None)
    return jax.shard_map(
        per_device, mesh=mesh, in_specs=in_specs, out_specs=out_specs, check_vma=False
    )
```

profile of v0, /device:TPU:15, one launch (start us, length us, event | category | flops | bytes accessed | tf_op | source)
XLA Modules:
  0.0 290.2 jit_solution(9980462576097650920)
XLA Ops:
  6.5 0.8 subtract_bitcast_fusion
  7.3 0.8 select_reduce_fusion.1
  8.6 0.7 copy.19
  9.3 5.7 %all-to-all-start.1 = ((s32[8,1,1]{2,1,0:T(1,128)}), s32[8,1,1]{2,1,0:T(1,128)S(1)}, u32[]{:S(2)}, u32[]{:S(2)}) async-start(s32[8,1,1]{2,1,0:T(1,128)} %copy.19), calls=%async_computation.1 | async-start | bytes 8192 | tf_op jit(solution)/shard_map/all_to_all | solution.py:60
  15.6 1.3 fusion.27
  16.9 0.7 copy.37
  17.6 0.6 broadcast.304
  18.2 3.6 %reduce.3 = bf16[448,448]{1,0:T(8,128)(2,1)S(1)} reduce(bf16[448,1,448]{2,1,0:T(2,128)(2,1)S(1)} %bitcast.33, bf16[]{:T(256)} %broadcast.304), dimensions={1}, to_apply=%bitcast.27.reduce_sub_computation | reduce | bytes 802818
  21.8 1.3 reshape.240
  23.1 4.8 %all-to-all-start = ((bf16[4,2,25088]{2,1,0:T(2,128)(2,1)}), bf16[4,2,25088]{2,1,0:T(2,128)(2,1)S(1)}, u32[]{:S(2)}, u32[]{:S(2)}) async-start(bf16[4,2,25088]{2,1,0:T(2,128)(2,1)} %reshape.240), calls=%async_computation | async-start | bytes 802816 | tf_op jit(solution)/shard_map/all_to_all | solution.py:69
  28.2 5.3 %all-to-all-done = bf16[4,2,25088]{2,1,0:T(2,128)(2,1)S(1)} async-done(((bf16[4,2,25088]{2,1,0:T(2,128)(2,1)}), bf16[4,2,25088]{2,1,0:T(2,128)(2,1)S(1)}, u32[]{:S(2)}, u32[]{:S(2)}) %all-to-all-start) | async-done | bytes 401440 | tf_op jit(solution)/shard_map/all_to_all | solution.py:69
  33.5 0.6 reshape.241
  34.3 0.6 gather_fusion.1
  35.1 25.9 %all_to_all.46 = bf16[8,112,448]{2,1,0:T(8,128)(2,1)} all-to-all(bf16[8,112,448]{2,1,0:T(8,128)(2,1)S(1)} %broadcast_select_fusion.5), channel_id=1, replica_groups=mesh['pairs'=8,'coup'=4] {'pairs'}, dimensions={0} | all-to-all | bytes 1605632 | tf_op jit(solution)/shard_map/all_to_all | solution.py:71
  61.0 0.7 all-gather.4.cloned.1.call-update
  62.0 31.6 %all-gather.6.cloned.1.call-done = bf16[8,448,448]{2,1,0:T(8,128)(2,1)} async-done(((bf16[8,112,448]{2,1,0:T(8,128)(2,1)}), bf16[8,448,448]{2,1,0:T(8,128)(2,1)}) %all-gather.6.cloned.1.call-update) | async-done | bytes 3211280 | tf_op jit(solution)/shard_map/all_gather | solution.py:72
  93.6 4.7 %gather_fusion.2 = bf16[8,448,448]{2,1,0:T(8,128)(2,1)} fusion(bf16[8,448,448]{2,1,0:T(8,128)(2,1)} %all-gather.6.cloned.1.call-done, s32[1024]{0:T(1024)S(1)} %pad_clamp_fusion), kind=kCustom, calls=%fused_computation.2.clone | custom fusion | bytes 6422560 | tf_op jit(solution)/shard_map/while/body/eval_jaxpr/jit(_take)/gather | solution.py:80
  98.3 49.2 %all-gather.4.cloned.1.call-done = bf16[16,448,448]{2,1,0:T(8,128)(2,1)} async-done(((bf16[4,448,448]{2,1,0:T(8,128)(2,1)}), bf16[16,448,448]{2,1,0:T(8,128)(2,1)}) %all-gather.4.cloned.1.call-update) | async-done | bytes 6422544 | tf_op jit(solution)/shard_map/all_gather | solution.py:45
  147.5 5.8 %gather_fusion = bf16[8,448,448]{2,1,0:T(8,128)(2,1)} fusion(bf16[16,448,448]{2,1,0:T(8,128)(2,1)} %all-gather.4.cloned.1.call-done, s32[1024]{0:T(1024)S(1)} %pad_clamp_fusion.2), kind=kCustom, calls=%fused_computation.clone | custom fusion | bytes 6422560 | tf_op jit(solution)/shard_map/while/body/eval_jaxpr/jit(_take)/gather | solution.py:81
  153.3 11.2 %fusion.10 = f32[8,448,448]{2,1,0:T(8,128)} fusion(bf16[8,448,448]{2,1,0:T(8,128)(2,1)} %gather_fusion.2, pred[8]{0:T(512)(128)(4,1)S(1)} %get-tuple-element.76, bf16[8,448,448]{2,1,0:T(8,128)(2,1)} %gather_fusion, pred[8]{0:T(512)(128)(4,1)S(1)} %get-tuple-element.77), kind=kOutput, calls=%fused_computation.15 | convolution fusion | flops 2883715072 | bytes 12845072 | tf_op jit(solution)/shard_map/while/body/eval_jaxpr/sac,sdc->sad/dot_general | solution.py:85
  164.5 13.6 %fusion.2 = f32[1,448,448]{2,0,1:T(1,128)S(1)} fusion(f32[8,448,448]{2,1,0:T(8,128)} %fusion.10, f32[8]{0:T(128)S(1)} %select_reduce_fusion.5, s32[8]{0:T(128)S(1)} %get-tuple-element.42, s32[]{:T(128)S(6)} %axis_index.25), kind=kOutput, calls=%fused_computation.7 | convolution fusion | flops 19267608 | bytes 7225412 | tf_op jit(solution)/shard_map/while/body/eval_jaxpr/ps,sad->pad/dot_general | solution.py:90
  178.4 0.7 copy.36
  179.1 3.6 %reduce.4 = bf16[448,448]{1,0:T(8,128)(2,1)S(1)} reduce(bf16[448,1,448]{2,1,0:T(2,128)(2,1)S(1)} %bitcast.34, bf16[]{:T(256)} %broadcast.304), dimensions={1}, to_apply=%bitcast.26.reduce_sub_computation | reduce | bytes 802818
  183.2 9.5 %all_to_all.47 = bf16[4,2,25088]{2,1,0:T(2,128)(2,1)S(1)} all-to-all(bf16[4,2,25088]{2,1,0:T(2,128)(2,1)S(1)} %reshape.242), channel_id=1, replica_groups=mesh['pairs'=8,'coup'=4] {'coup'}, dimensions={0} | all-to-all | bytes 802816 | tf_op jit(solution)/shard_map/all_to_all | solution.py:69
  192.8 0.6 reshape.243
  193.5 0.6 gather_fusion.3
  194.3 25.9 %all_to_all.48 = bf16[8,112,448]{2,1,0:T(8,128)(2,1)} all-to-all(bf16[8,112,448]{2,1,0:T(8,128)(2,1)S(1)} %broadcast_select_fusion.6), channel_id=1, replica_groups=mesh['pairs'=8,'coup'=4] {'pairs'}, dimensions={0} | all-to-all | bytes 1605632 | tf_op jit(solution)/shard_map/all_to_all | solution.py:71
  220.2 32.8 %all-gather.8.cloned.1.call-done = bf16[8,448,448]{2,1,0:T(8,128)(2,1)} async-done(((bf16[8,112,448]{2,1,0:T(8,128)(2,1)}), bf16[8,448,448]{2,1,0:T(8,128)(2,1)}) %all-gather.8.cloned.1.call-update) | async-done | bytes 3211280 | tf_op jit(solution)/shard_map/all_gather | solution.py:72
  253.1 4.7 %gather_fusion.4 = bf16[8,448,448]{2,1,0:T(8,128)(2,1)} fusion(bf16[8,448,448]{2,1,0:T(8,128)(2,1)} %all-gather.8.cloned.1.call-done, s32[1024]{0:T(1024)S(1)} %pad_clamp_fusion), kind=kCustom, calls=%fused_computation.4.clone | custom fusion | bytes 6422560 | tf_op jit(solution)/shard_map/while/body/eval_jaxpr/jit(_take)/gather | solution.py:80
  257.8 11.2 %fusion.8 = f32[8,448,448]{2,1,0:T(8,128)} fusion(bf16[8,448,448]{2,1,0:T(8,128)(2,1)} %gather_fusion.4, pred[8]{0:T(512)(128)(4,1)S(1)} %get-tuple-element.76, bf16[8,448,448]{2,1,0:T(8,128)(2,1)} %gather_fusion, pred[8]{0:T(512)(128)(4,1)S(1)} %get-tuple-element.77), kind=kOutput, calls=%fused_computation.13 | convolution fusion | flops 2883715072 | bytes 12845072 | tf_op jit(solution)/shard_map/while/body/eval_jaxpr/sac,sdc->sad/dot_general | solution.py:85
  269.0 13.5 %fusion = f32[1,448,448]{2,0,1:T(1,128)S(1)} fusion(f32[8,448,448]{2,1,0:T(8,128)} %fusion.8, f32[8]{0:T(128)S(1)} %select_reduce_fusion.5, s32[8]{0:T(128)S(1)} %get-tuple-element.42, s32[]{:T(128)S(6)} %axis_index.25), kind=kOutput, calls=%fused_computation.5 | convolution fusion | flops 19267608 | bytes 7225412 | tf_op jit(solution)/shard_map/while/body/eval_jaxpr/ps,sad->pad/dot_general | solution.py:90
  282.5 1.2 fusion.32
  (34 shorter events, 2.2 us)
Async XLA Ops:
  9.3 13.8 %all-to-all-start.1 = ((s32[8,1,1]{2,1,0:T(1,128)}), s32[8,1,1]{2,1,0:T(1,128)S(1)}, u32[]{:S(2)}, u32[]{:S(2)}) async-start(s32[8,1,1]{2,1,0:T(1,128)} %copy.19), calls=%async_computation.1 | async-start | bytes 8192 | tf_op jit(solution)/shard_map/all_to_all | solution.py:60
  23.1 10.5 %all-to-all-start = ((bf16[4,2,25088]{2,1,0:T(2,128)(2,1)}), bf16[4,2,25088]{2,1,0:T(2,128)(2,1)S(1)}, u32[]{:S(2)}, u32[]{:S(2)}) async-start(bf16[4,2,25088]{2,1,0:T(2,128)(2,1)} %reshape.240), calls=%async_computation | async-start | bytes 802816 | tf_op jit(solution)/shard_map/all_to_all | solution.py:69
  27.9 65.7 %all-gather.6.cloned.1.call-start = ((), (), s32[]{:S(2)}) async-start(), calls=%async_computation.6 | async-start | bytes 4587520 | tf_op jit(solution)/shard_map/all_gather | solution.py:72
  34.9 26.9 %copy-start.2 = (f32[16]{0:T(128)S(1)}, f32[16]{0:T(128)}, u32[]{:S(2)}) copy-start(f32[16]{0:T(128)} %param.15) | copy-start | bytes 196
  61.0 86.6 %all-gather.4.cloned.1.call-start = ((), (), s32[]{:S(2)}) async-start(), calls=%async_computation.5 | async-start | bytes 9175040 | tf_op jit(solution)/shard_map/all_gather | solution.py:45
  61.7 191.3 %all-gather.8.cloned.1.call-start = ((), (), s32[]{:S(2)}) async-start(), calls=%async_computation.7 | async-start | bytes 4587520 | tf_op jit(solution)/shard_map/all_gather | solution.py:72
  164.5 13.6 %copy-start = (bf16[1,448,448]{2,1,0:T(8,128)(2,1)S(1)}, bf16[1,448,448]{2,1,0:T(8,128)(2,1)}, u32[]{:S(2)}) copy-start(bf16[1,448,448]{2,1,0:T(8,128)(2,1)} %param.16) | copy-start | bytes 1204228
  164.5 13.6 %copy-start.1 = (f32[1,448]{1,0:T(1,128)S(1)}, f32[1,448]{1,0:T(1,128)}, u32[]{:S(2)}) copy-start(f32[1,448]{1,0:T(1,128)} %param.17) | copy-start | bytes 5380
Sparse Core Ops, SparseCore 0:
  61.1 32.4 all-gather.5
  95.1 52.3 all-gather.3
  220.3 32.6 all-gather.7
where the time goes:
time: 293 us; the launch traced here: 290 us
  waiting for transfers between devices  120 us (41%)
  blocking collectives  61.3 us (21%)
  matrix products  49.5 us (17%)
  local copies, waits for them, and re-layouts  22.5 us (8%)
  between operations  14 us (5%)
  other arithmetic  12.6 us (4%)
  starting transfers between devices  10.6 us (4%)
    all_gather x2, waiting for transfers between devices, per_device(): fetched = lax.all_gather(arrived, 'coup', axis=1, tiled=True)  64.5 us
    all_to_all x2, blocking collectives, per_device(): lax.all_to_all(outgoing, 'pairs', split_axis=0, concat_axis=0, tiled=True)  51.8 us
    all_gather x1, waiting for transfers between devices, per_device(): ovl_table = lax.all_gather(intersections, 'coup', axis=0, tiled=True)  49.2 us
    dot_general x2, matrix products, accumulate(): jnp.einsum('ps,sad->pad', spread, full_product, precision=lax.Precision.H...  27.1 us
    dot_general x2, matrix products, accumulate(): jnp.einsum('sac,sdc->sad', left_product, ovl_block, preferred_element_typ...  22.4 us
    all_to_all x1, blocking collectives, per_device(): lax.all_to_all(rounded, 'coup', split_axis=1, concat_axis=0, tiled=True)  9.54 us
    gather x2, local copies, waits for them, and re-layouts, accumulate(): amp_block = jnp.take(fetched, source_block, axis=0)  9.47 us
    unnamed x2, other arithmetic  7.23 us
  transfers between devices with their start and end apart: 5, of which 4 were waited for; matrix products, arithmetic and copies ran while one was open for 4% of the time, Pallas kernels for 0%

commit v1 on v0

v1 whole, which is shorter than its diff:
```python
import functools

import jax
import jax.numpy as jnp
from jax import lax
from jax.experimental import pallas as pl
from jax.experimental.pallas import tpu as pltpu
from jax.sharding import PartitionSpec as P

ITERS = 2
MESH = pl.DeviceIdType.MESH
VMEM_LIMIT = 48 * 1024 * 1024


def lookup(lookup_table, queries):
    columns = lax.broadcasted_iota(jnp.int32, (queries.shape[0], lookup_table.shape[0]), 1)
    return jnp.sum(jnp.where(queries[:, None] == columns, lookup_table[None, :], 0), axis=1)


def remote(src, dst, send_sem, recv_sem, device_id):
    copy = pltpu.make_async_remote_copy(
        src_ref=src, dst_ref=dst, send_sem=send_sem, recv_sem=recv_sem,
        device_id=device_id, device_id_type=MESH,
    )
    copy.start()
    return copy


def send_strips(amp_ref, strips, send_sem, recv_sem, m, coup_total):
    rows = strips.shape[2]
    copies = []
    for d in range(1, coup_total):
        q = lax.rem(m + d, coup_total)
        copies.append(remote(
            amp_ref.at[:, pl.ds(pl.multiple_of(q * rows, 16), rows), :],
            strips.at[m], send_sem.at[d], recv_sem.at[d], {"coup": q},
        ))
    strips[m] = amp_ref[:, pl.ds(pl.multiple_of(m * rows, 16), rows), :]
    return copies


def send_picks(wanted, strips, outbuf, arrived, send_sem, recv_sem, g, group_total):
    pair_dev = strips.shape[1]
    copies = []
    for d in list(range(1, group_total)) + [0]:
        h = lax.rem(g + d, group_total)
        pick = wanted[h, 0, 0]
        if pair_dev == 1:
            block = strips[pick, 0]
        else:
            block = strips[pick // pair_dev, pick % pair_dev]
        if d == 0:
            arrived[g] = block
        else:
            outbuf[d] = block
            copies.append(remote(
                outbuf.at[d], arrived.at[g], send_sem.at[d], recv_sem.at[d], {"pairs": h}
            ))
    return copies


def greet(coords_list):
    barrier = pltpu.get_barrier_semaphore()
    for coords in coords_list:
        pl.semaphore_signal(barrier, inc=1, device_id=coords, device_id_type=MESH)
    pl.semaphore_wait(barrier, len(coords_list))


def first_exchange(
    group_total, coup_total, amp_ref, ask_ref, x_ref, arrived, x_all, asked, strips, outbuf, wanted,
    strip_send, strip_recv, ask_send, ask_recv, pick_send, pick_recv,
    far_send, far_recv, sib_send, sib_recv, fwd_send, fwd_recv, local_sem, want_sem,
):
    g, m = lax.axis_index("pairs"), lax.axis_index("coup")
    ov_dev = x_ref.shape[0]
    chips = coup_total // 2
    chip, core = m // 2, lax.rem(m, 2)
    sibling = chip * 2 + 1 - core
    greet(
        [{"coup": lax.rem(m + d, coup_total)} for d in range(1, coup_total)]
        + [{"pairs": lax.rem(g + d, group_total)} for d in range(1, group_total)]
    )
    strip_copies = send_strips(amp_ref, strips, strip_send, strip_recv, m, coup_total)
    ask_copies = []
    for d in range(1, group_total):
        h = lax.rem(g + d, group_total)
        ask_copies.append(remote(
            ask_ref.at[h], asked.at[g], ask_send.at[d], ask_recv.at[d], {"pairs": h}
        ))
    asked[g] = ask_ref[g]
    far_copies = []
    for i in range(ov_dev):
        for d in range(1, chips):
            peer = lax.rem(chip + d, chips) * 2 + core
            far_copies.append((d, i, remote(
                x_ref.at[i], x_all.at[m * ov_dev + i],
                far_send.at[d, i], far_recv.at[d, i], {"coup": peer},
            )))
    sib_copy = remote(
        x_ref, x_all.at[pl.ds(m * ov_dev, ov_dev)], sib_send, sib_recv, {"coup": sibling}
    )
    own_copy = pltpu.make_async_copy(x_ref, x_all.at[pl.ds(m * ov_dev, ov_dev)], local_sem)
    own_copy.start()
    for copy in ask_copies:
        copy.wait_recv()
    want_copy = pltpu.make_async_copy(asked, wanted, want_sem)
    want_copy.start()
    want_copy.wait()
    for copy in strip_copies:
        copy.wait_recv()
    pick_copies = send_picks(
        wanted, strips, outbuf, arrived, pick_send, pick_recv, g, group_total
    )
    forwards = []
    for d, i, copy in far_copies:
        copy.wait_recv()
        origin = lax.rem(chip - d + chips, chips) * 2 + core
        slot = x_all.at[origin * ov_dev + i]
        forwards.append(remote(
            slot, slot, fwd_send.at[d, i], fwd_recv.at[d, i], {"coup": sibling}
        ))
    own_copy.wait()
    sib_copy.wait()
    for copy in forwards + pick_copies:
        copy.wait()
    for copy in strip_copies + ask_copies + [c for _, _, c in far_copies]:
        copy.wait_send()


def later_exchange(
    group_total, coup_total, amp_ref, wanted, arrived, strips, outbuf,
    strip_send, strip_recv, pick_send, pick_recv,
):
    g, m = lax.axis_index("pairs"), lax.axis_index("coup")
    greet(
        [{"coup": lax.rem(m + d, coup_total)} for d in range(1, coup_total)]
        + [{"pairs": lax.rem(g + d, group_total)} for d in range(1, group_total)]
    )
    strip_copies = send_strips(amp_ref, strips, strip_send, strip_recv, m, coup_total)
    for copy in strip_copies:
        copy.wait_recv()
    pick_copies = send_picks(
        wanted, strips, outbuf, arrived, pick_send, pick_recv, g, group_total
    )
    for copy in pick_copies:
        copy.wait()
    for copy in strip_copies:
        copy.wait_send()


def reduce_partials(
    coup_total, part, total, near, joined, far, near_send, near_recv, far_send, far_recv
):
    m = lax.axis_index("coup")
    chips = coup_total // 2
    chip, core = m // 2, lax.rem(m, 2)
    sibling = chip * 2 + 1 - core
    peers = [lax.rem(chip + d, chips) * 2 for d in range(chips)]
    greet([{"coup": sibling}] + [{"coup": peers[d] + core} for d in range(1, chips)])
    order = list(range(1, chips)) + [0]
    near_copies = {}
    for d in order:
        near_copies[d] = remote(
            part.at[peers[d] + 1 - core], near.at[d], near_send.at[d], near_recv.at[d],
            {"coup": sibling},
        )
    far_copies = []
    for d in order:
        near_copies[d].wait_recv()
        both = part[peers[d] + core].astype(jnp.float32) + near[d].astype(jnp.float32)
        if d == 0:
            total[...] = both
        else:
            joined[d] = both.astype(jnp.bfloat16)
            far_copies.append((d, remote(
                joined.at[d], far.at[d], far_send.at[d], far_recv.at[d],
                {"coup": peers[d] + core},
            )))
    for d, copy in far_copies:
        copy.wait()
        total[...] += far[d].astype(jnp.float32)
    for d in order:
        near_copies[d].wait_send()


def couple(x_index, source, owner, member, weight, amp_ref, x_ref, out_ref, acc, padded):
    k = pl.program_id(0)
    rows = amp_ref.shape[1]

    @pl.when(k == 0)
    def _():
        acc[...] = jnp.zeros_like(acc)
        padded[...] = jnp.zeros_like(padded)

    x = x_ref[0]
    right = lax.dot_general(
        amp_ref[source[k]], x, (((1,), (1,)), ((), ())), preferred_element_type=jnp.float32
    )
    padded[pl.ds(pl.multiple_of(member[0] * rows, 16), rows), :] = (
        right * weight[k]
    ).astype(jnp.bfloat16)
    acc[owner[k]] += jnp.dot(x, padded[...], preferred_element_type=jnp.float32)

    @pl.when(k == pl.num_programs(0) - 1)
    def _():
        for p in range(acc.shape[0]):
            out_ref[p] = acc[p].astype(jnp.bfloat16)


def per_device(
    coupling_list, pair_slot, coupling_weight, integrals, orbital_energy, pair_energy, intersections
):
    group_total = lax.axis_size("pairs")
    coup_total = lax.axis_size("coup")
    group_index = lax.axis_index("pairs")
    member = lax.axis_index("coup")
    pair_dev, width = integrals.shape[0], integrals.shape[-1]
    ov_dev = intersections.shape[0]
    group_pairs = pair_dev * coup_total
    couplings = coupling_list.shape[1]
    rows = width // coup_total
    chips = coup_total // 2

    owner_row = lookup(pair_slot, coupling_list[0])
    reader_row = lookup(pair_slot, coupling_list[1])
    owner = owner_row - group_index * group_pairs
    source = reader_row // group_pairs
    x_index = coupling_list[2] - group_index * (ov_dev * coup_total)
    sources = lax.broadcasted_iota(jnp.int32, (group_total, couplings), 0)
    ask = jnp.max(
        jnp.where(source[None, :] == sources, (reader_row % group_pairs)[None, :], 0), axis=1
    )
    ask = jnp.broadcast_to(ask[:, None, None], (group_total, 8, 128))

    denominator = (
        orbital_energy[:, :, None] + orbital_energy[:, None, :] + pair_energy[:, None, None]
    )
    integral_f = integrals.astype(jnp.float32)
    rounded = (-integral_f / denominator).astype(jnp.bfloat16)

    vmem = pl.BlockSpec(memory_space=pltpu.VMEM)
    smem = pl.BlockSpec(memory_space=pltpu.SMEM)
    anywhere = pl.BlockSpec(memory_space=pl.ANY)
    dma = pltpu.SemaphoreType.DMA
    arrived_shape = jax.ShapeDtypeStruct((group_total, rows, width), jnp.bfloat16)
    strips_scratch = pltpu.VMEM((coup_total, pair_dev, rows, width), jnp.bfloat16)
    out_scratch = pltpu.VMEM((group_total, rows, width), jnp.bfloat16)

    def params(collective_id):
        return pltpu.CompilerParams(
            collective_id=collective_id, has_side_effects=True, vmem_limit_bytes=VMEM_LIMIT
        )

    arrived, x_all, asked = pl.pallas_call(
        functools.partial(first_exchange, group_total, coup_total),
        out_shape=(
            arrived_shape,
            jax.ShapeDtypeStruct((ov_dev * coup_total, width, width), jnp.bfloat16),
            jax.ShapeDtypeStruct((group_total, 8, 128), jnp.int32),
        ),
        in_specs=[vmem, vmem, anywhere],
        out_specs=(vmem, anywhere, vmem),
        scratch_shapes=[
            strips_scratch, out_scratch, pltpu.SMEM((group_total, 8, 128), jnp.int32),
            dma((coup_total,)), dma((coup_total,)), dma((group_total,)), dma((group_total,)),
            dma((group_total,)), dma((group_total,)),
            dma((chips, ov_dev)), dma((chips, ov_dev)), dma, dma,
            dma((chips, ov_dev)), dma((chips, ov_dev)), dma, dma,
        ],
        compiler_params=params(0),
        name="first_exchange",
    )(rounded, ask, intersections)

    for iteration in range(ITERS):
        if iteration > 0:
            arrived = pl.pallas_call(
                functools.partial(later_exchange, group_total, coup_total),
                out_shape=arrived_shape,
                in_specs=[vmem, smem],
                out_specs=vmem,
                scratch_shapes=[
                    strips_scratch, out_scratch,
                    dma((coup_total,)), dma((coup_total,)), dma((group_total,)), dma((group_total,)),
                ],
                compiler_params=params(1),
                name="later_exchange",
            )(rounded, asked)
        part = pl.pallas_call(
            couple,
            out_shape=jax.ShapeDtypeStruct((group_pairs, width, width), jnp.bfloat16),
            grid_spec=pltpu.PrefetchScalarGridSpec(
                num_scalar_prefetch=4,
                grid=(couplings,),
                in_specs=[
                    smem,
                    pl.BlockSpec((group_total, rows, width), lambda k, *_: (0, 0, 0)),
                    pl.BlockSpec((1, width, width), lambda k, xi, *_: (xi[k], 0, 0)),
                ],
                out_specs=pl.BlockSpec((group_pairs, width, width), lambda k, *_: (0, 0, 0)),
                scratch_shapes=[
                    pltpu.VMEM((group_pairs, width, width), jnp.float32),
                    pltpu.VMEM((width, width), jnp.bfloat16),
                ],
            ),
            compiler_params=pltpu.CompilerParams(vmem_limit_bytes=VMEM_LIMIT),
            name="couple",
        )(x_index, source, owner, member[None], coupling_weight, arrived, x_all)
        block = (pair_dev, width, width)
        coupled = pl.pallas_call(
            functools.partial(reduce_partials, coup_total),
            out_shape=jax.ShapeDtypeStruct(block, jnp.float32),
            in_specs=[vmem],
            out_specs=vmem,
            scratch_shapes=[
                pltpu.VMEM((chips,) + block, jnp.bfloat16),
                pltpu.VMEM((chips,) + block, jnp.bfloat16),
                pltpu.VMEM((chips,) + block, jnp.bfloat16),
                dma((chips,)), dma((chips,)), dma((chips,)), dma((chips,)),
            ],
            compiler_params=params(2),
            name="reduce_partials",
        )(part.reshape((coup_total,) + block))
        amplitudes = -(integral_f + coupled) / denominator
        rounded = amplitudes.astype(jnp.bfloat16)
    return amplitudes


def solution(mesh):
    in_specs = (
        P(None, "pairs"),
        P(),
        P("pairs"),
        P(("pairs", "coup"), None, None),
        P(("pairs", "coup"), None),
        P(("pairs", "coup")),
        P(("pairs", "coup"), None, None),
    )
    out_specs = P(("pairs", "coup"), None, None)
    return jax.shard_map(
        per_device, mesh=mesh, in_specs=in_specs, out_specs=out_specs, check_vma=False
    )
```

time: 293 us -> 151 us (0.52)
  Pallas kernels: 0 us -> 144 us
  waiting for transfers between devices: 120 us -> 0 us
  blocking collectives: 61.3 us -> 0 us
  matrix products: 49.5 us -> 0 us
  local copies, waits for them, and re-layouts: 22.5 us -> 1.59 us
  between operations: 14 us -> 0.78 us
  starting transfers between devices: 10.6 us -> 0 us
  other arithmetic: 12.6 us -> 4.48 us
    pallas_call x0 -> x6, Pallas kernels: none -> 144 us  [the longest x1 50.9 us: per_device(): pl.pallas_call(functools.partial(first_exchange, group_total, coup_total)...]
    all_gather x3 -> x0, waiting for transfers between devices: 114 us -> none  [the longest x2 64.5 us: per_device(): fetched = lax.all_gather(arrived, 'coup', axis=1, tiled=True)]
    all_to_all x3 -> x0, blocking collectives: 61.3 us -> none  [the longest x2 51.8 us: per_device(): lax.all_to_all(outgoing, 'pairs', split_axis=0, concat_axis=0, tiled=True)]
    dot_general x4 -> x0, matrix products: 49.5 us -> none  [the longest x2 27.1 us: accumulate(): jnp.einsum('ps,sad->pad', spread, full_product, precision=lax.Precision.H...]
    gather x5 -> x0, local copies, waits for them, and re-layouts: 16.4 us -> none  [the longest x2 9.47 us: accumulate(): amp_block = jnp.take(fetched, source_block, axis=0)]
    all_to_all x2 -> x0, starting transfers between devices: 10.5 us -> none  [the longest x1 5.66 us: per_device(): lax.all_to_all(wanted_here, 'pairs', split_axis=0, concat_axis=0, tiled=T...]
    unnamed x2 -> x0, other arithmetic: 7.23 us -> none
    all_to_all x2 -> x0, waiting for transfers between devices: 5.35 us -> none  [the longest x1 5.35 us: per_device(): lax.all_to_all(rounded, 'coup', split_axis=1, concat_axis=0, tiled=True)]
  transfers between devices with their start and end apart: 5 -> 0, of which waited for: 4 -> 0; matrix products, arithmetic and copies ran while one was open for 4% -> 0% of each run, Pallas kernels for 0% -> 0%
where the time goes in v1:
time: 151 us
  Pallas kernels  144 us (95%)
  other arithmetic  4.48 us (3%)
  local copies, waits for them, and re-layouts  1.59 us (1%)
    pallas_call x1, Pallas kernels, per_device(): pl.pallas_call(functools.partial(first_exchange, group_total, coup_total)...  50.9 us
    pallas_call x1, Pallas kernels, per_device(): pl.pallas_call(functools.partial(later_exchange, group_total, coup_total)...  32.1 us
    pallas_call x2, Pallas kernels, per_device(): pl.pallas_call(couple, out_shape=jax.ShapeDtypeStruct((group_pairs, width...  31.8 us
    pallas_call x2, Pallas kernels, per_device(): pl.pallas_call(functools.partial(reduce_partials, coup_total), out_shape=...  28.9 us

profile of v1, /device:TPU:15, one launch (start us, length us, event | category | flops | bytes accessed | tf_op | source)
XLA Modules:
  0.0 150.5 jit_solution(4197365302690475863)
XLA Ops:
  0.0 0.0 copy-start.1
  0.7 0.8 slice_bitcast_fusion.1
  1.5 0.8 select_reduce_fusion
  2.3 0.1 select_reduce_fusion.2
  2.4 0.1 broadcast_in_dim.50.ask_ref
  2.5 1.3 fusion.1.amp_ref
  3.8 0.0 copy-start
  3.8 1.5 copy-done
  5.3 50.9 %first_exchange.1 = (bf16[8,112,448]{2,1,0:T(8,128)(2,1)S(1)}, bf16[16,448,448]{2,1,0:T(8,128)(2,1)}, s32[8,8,128]{2,1,0:T(8,128)S(1)}) custom-call(bf16[1,448,448]{2,1,0:T(8,128)(2,1)S(1)} %fusion.1.amp_ref, s32[8,8,128]{2,1,0:T(8,128)S(1)} %broadcast_in_dim.50.ask_ref, bf16[4,448,448]{2,1,0:T(8,128)(2,1)S(1)} %copy-done), custom_call_target="tpu_custom_call" | custom-call | tf_op jit(solution)/shard_map/first_exchange/pallas_call | solution.py:254
  56.2 0.0 copy-done.1
  56.2 15.9 %couple.2 = bf16[4,448,448]{2,1,0:T(8,128)(2,1)S(1)} custom-call(s32[16]{0:T(128)S(1)} %get-tuple-element.14.x_index, s32[16]{0:T(128)S(1)} %get-tuple-element.17.source, s32[16]{0:T(128)S(1)} %get-tuple-element.18.owner, s32[1]{0:T(128)} %bitcast.3.member, f32[16]{0:T(128)S(1)} %copy-done.1, bf16[8,112,448]{2,1,0:T(8,128)(2,1)S(1)} %get-tuple-element.8.amp_ref, ...), custom_call_target="tpu_custom_call" | custom-call | tf_op jit(solution)/shard_map/couple/pallas_call | solution.py:288
  72.2 0.0 copy-start.2
  72.2 0.0 copy-start.3
  72.2 14.3 %reduce_partials.2 = f32[1,448,448]{2,1,0:T(8,128)S(1)} custom-call(bf16[4,1,448,448]{3,2,1,0:T(8,128)(2,1)S(1)} %bitcast.15), custom_call_target="tpu_custom_call" | custom-call | tf_op jit(solution)/shard_map/reduce_partials/pallas_call | solution.py:309
  86.5 0.0 copy-done.2
  86.5 0.0 copy-done.3
  86.5 0.3 fusion.4.amp_ref
  86.8 32.1 %later_exchange.1.amp_ref = bf16[8,112,448]{2,1,0:T(8,128)(2,1)S(1)} custom-call(bf16[1,448,448]{2,1,0:T(8,128)(2,1)S(1)} %fusion.4.amp_ref, s32[8,8,128]{2,1,0:T(8,128)S(1)} %get-tuple-element.10.wanted), custom_call_target="tpu_custom_call" | custom-call | tf_op jit(solution)/shard_map/later_exchange/pallas_call | solution.py:276
  118.9 15.9 %couple.3 = bf16[4,448,448]{2,1,0:T(8,128)(2,1)S(1)} custom-call(s32[16]{0:T(128)S(1)} %get-tuple-element.14.x_index, s32[16]{0:T(128)S(1)} %get-tuple-element.17.source, s32[16]{0:T(128)S(1)} %get-tuple-element.18.owner, s32[1]{0:T(128)} %bitcast.3.member, f32[16]{0:T(128)S(1)} %copy-done.1, bf16[8,112,448]{2,1,0:T(8,128)(2,1)S(1)} %later_exchange.1.amp_ref, ...), custom_call_target="tpu_custom_call" | custom-call | tf_op jit(solution)/shard_map/couple/pallas_call | solution.py:288
  134.8 14.6 %reduce_partials.3 = f32[1,448,448]{2,1,0:T(8,128)S(1)} custom-call(bf16[4,1,448,448]{3,2,1,0:T(8,128)(2,1)S(1)} %bitcast.14), custom_call_target="tpu_custom_call" | custom-call | tf_op jit(solution)/shard_map/reduce_partials/pallas_call | solution.py:309
  149.4 1.2 fusion.6
  (1 shorter events, 0.0 us)
Async XLA Ops:
  0.0 56.2 %copy-start.1 = (f32[16]{0:T(128)S(1)}, f32[16]{0:T(128)}, u32[]{:S(2)}) copy-start(f32[16]{0:T(128)} %weight.3) | copy-start | bytes 196
  3.8 1.5 copy-start
  72.2 14.3 %copy-start.2 = (bf16[1,448,448]{2,1,0:T(8,128)(2,1)S(1)}, bf16[1,448,448]{2,1,0:T(8,128)(2,1)}, u32[]{:S(2)}) copy-start(bf16[1,448,448]{2,1,0:T(8,128)(2,1)} %param.10) | copy-start | bytes 1204228
  72.2 14.3 %copy-start.3 = (f32[1,448]{1,0:T(1,128)S(1)}, f32[1,448]{1,0:T(1,128)}, u32[]{:S(2)}) copy-start(f32[1,448]{1,0:T(1,128)} %param.11) | copy-start | bytes 5380

commit v2 on v1

--- a/solution.py
+++ b/solution.py
@@ -1,4 +1,5 @@
 import functools
+import math
 
 import jax
 import jax.numpy as jnp
@@ -149,57 +150,72 @@
 
 
 def reduce_partials(
-    coup_total, part, total, near, joined, far, near_send, near_recv, far_send, far_recv
+    coup_total, chunks, part, total, near, joined, far, near_send, near_recv, far_send, far_recv
 ):
     m = lax.axis_index("coup")
     chips = coup_total // 2
     chip, core = m // 2, lax.rem(m, 2)
     sibling = chip * 2 + 1 - core
     peers = [lax.rem(chip + d, chips) * 2 for d in range(chips)]
+    size = total.shape[1] // chunks
+    rows = [slice(c * size, (c + 1) * size) for c in range(chunks)]
+    order = [(d, c) for d in list(range(1, chips)) + [0] for c in range(chunks)]
     greet([{"coup": sibling}] + [{"coup": peers[d] + core} for d in range(1, chips)])
-    order = list(range(1, chips)) + [0]
     near_copies = {}
-    for d in order:
-        near_copies[d] = remote(
-            part.at[peers[d] + 1 - core], near.at[d], near_send.at[d], near_recv.at[d],
-            {"coup": sibling},
+    for d, c in order:
+        near_copies[d, c] = remote(
+            part.at[peers[d] + 1 - core, :, rows[c]], near.at[d, :, rows[c]],
+            near_send.at[d, c], near_recv.at[d, c], {"coup": sibling},
         )
     far_copies = []
-    for d in order:
-        near_copies[d].wait_recv()
-        both = part[peers[d] + core].astype(jnp.float32) + near[d].astype(jnp.float32)
+    for d, c in order:
+        near_copies[d, c].wait_recv()
+        both = part[peers[d] + core, :, rows[c]].astype(jnp.float32)
+        both += near[d, :, rows[c]].astype(jnp.float32)
         if d == 0:
-            total[...] = both
+            total[:, rows[c]] = both
         else:
-            joined[d] = both.astype(jnp.bfloat16)
-            far_copies.append((d, remote(
-                joined.at[d], far.at[d], far_send.at[d], far_recv.at[d],
-                {"coup": peers[d] + core},
+            joined[d, :, rows[c]] = both.astype(jnp.bfloat16)
+            far_copies.append((d, c, remote(
+                joined.at[d, :, rows[c]], far.at[d, :, rows[c]],
+                far_send.at[d, c], far_recv.at[d, c], {"coup": peers[d] + core},
             )))
-    for d, copy in far_copies:
-        copy.wait()
-        total[...] += far[d].astype(jnp.float32)
-    for d in order:
-        near_copies[d].wait_send()
-
-
-def couple(x_index, source, owner, member, weight, amp_ref, x_ref, out_ref, acc, padded):
+    for d, c, copy in far_copies:
+        copy.wait_recv()
+        total[:, rows[c]] += far[d, :, rows[c]].astype(jnp.float32)
+    for _, _, copy in far_copies:
+        copy.wait_send()
+    for d, c in order:
+        near_copies[d, c].wait_send()
+
+
+def couple(coup_total, batch, x_index, source, owner, member, weight, amp_ref, *refs):
+    x_refs, (out_ref, acc, padded) = refs[:batch], refs[batch:]
     k = pl.program_id(0)
-    rows = amp_ref.shape[1]
+    rows, width = amp_ref.shape[1:]
 
     @pl.when(k == 0)
     def _():
         acc[...] = jnp.zeros_like(acc)
         padded[...] = jnp.zeros_like(padded)
 
-    x = x_ref[0]
-    right = lax.dot_general(
-        amp_ref[source[k]], x, (((1,), (1,)), ((), ())), preferred_element_type=jnp.float32
-    )
-    padded[pl.ds(pl.multiple_of(member[0] * rows, 16), rows), :] = (
-        right * weight[k]
-    ).astype(jnp.bfloat16)
-    acc[owner[k]] += jnp.dot(x, padded[...], preferred_element_type=jnp.float32)
+    def step(low):
+        first = low // 128 * 128
+        last = min(pl.cdiv(low + rows, 128) * 128, width)
+        for b in range(batch):
+            right = lax.dot_general(
+                amp_ref[source[k * batch + b]], x_refs[b][0],
+                (((1,), (1,)), ((), ())), preferred_element_type=jnp.float32,
+            )
+            padded[b, low:low + rows] = (right * weight[k * batch + b]).astype(jnp.bfloat16)
+        for b in range(batch):
+            acc[owner[k * batch + b]] += jnp.dot(
+                x_refs[b][0, :, first:last], padded[b, first:last],
+                preferred_element_type=jnp.float32,
+            )
+
+    for q in range(coup_total):
+        pl.when(member[0] == q)(functools.partial(step, q * rows))
 
     @pl.when(k == pl.num_programs(0) - 1)
     def _():
@@ -220,6 +236,8 @@
     couplings = coupling_list.shape[1]
     rows = width // coup_total
     chips = coup_total // 2
+    batch = math.gcd(couplings, 4)
+    chunks = math.gcd(width // 16, 4)
 
     owner_row = lookup(pair_slot, coupling_list[0])
     reader_row = lookup(pair_slot, coupling_list[1])
@@ -286,28 +304,30 @@
                 name="later_exchange",
             )(rounded, asked)
         part = pl.pallas_call(
-            couple,
+            functools.partial(couple, coup_total, batch),
             out_shape=jax.ShapeDtypeStruct((group_pairs, width, width), jnp.bfloat16),
             grid_spec=pltpu.PrefetchScalarGridSpec(
                 num_scalar_prefetch=4,
-                grid=(couplings,),
+                grid=(couplings // batch,),
                 in_specs=[
                     smem,
                     pl.BlockSpec((group_total, rows, width), lambda k, *_: (0, 0, 0)),
-                    pl.BlockSpec((1, width, width), lambda k, xi, *_: (xi[k], 0, 0)),
+                ] + [
+                    pl.BlockSpec((1, width, width), lambda k, xi, *_, b=b: (xi[k * batch + b], 0, 0))
+                    for b in range(batch)
                 ],
                 out_specs=pl.BlockSpec((group_pairs, width, width), lambda k, *_: (0, 0, 0)),
                 scratch_shapes=[
                     pltpu.VMEM((group_pairs, width, width), jnp.float32),
-                    pltpu.VMEM((width, width), jnp.bfloat16),
+                    pltpu.VMEM((batch, width, width), jnp.bfloat16),
                 ],
             ),
             compiler_params=pltpu.CompilerParams(vmem_limit_bytes=VMEM_LIMIT),
             name="couple",
-        )(x_index, source, owner, member[None], coupling_weight, arrived, x_all)
+        )(x_index, source, owner, member[None], coupling_weight, arrived, *[x_all] * batch)
         block = (pair_dev, width, width)
         coupled = pl.pallas_call(
-            functools.partial(reduce_partials, coup_total),
+            functools.partial(reduce_partials, coup_total, chunks),
             out_shape=jax.ShapeDtypeStruct(block, jnp.float32),
             in_specs=[vmem],
             out_specs=vmem,
@@ -315,7 +335,7 @@
                 pltpu.VMEM((chips,) + block, jnp.bfloat16),
                 pltpu.VMEM((chips,) + block, jnp.bfloat16),
                 pltpu.VMEM((chips,) + block, jnp.bfloat16),
-                dma((chips,)), dma((chips,)), dma((chips,)), dma((chips,)),
+                *[dma((chips, chunks))] * 4,
             ],
             compiler_params=params(2),
             name="reduce_partials",

time: 151 us -> 134 us (0.89)
  Pallas kernels: 144 us -> 127 us
    pallas_call x4, Pallas kernels: 60.7 us -> 43.7 us  [the longest x2 28.2 us: per_device(): pl.pallas_call(functools.partial(reduce_partials, coup_total, chunks), ou...]
where the time goes in v2:
time: 134 us
  Pallas kernels  127 us (95%)
  other arithmetic  4.48 us (3%)
  local copies, waits for them, and re-layouts  1.59 us (1%)
    pallas_call x1, Pallas kernels, per_device(): pl.pallas_call(functools.partial(first_exchange, group_total, coup_total)...  50.9 us
    pallas_call x1, Pallas kernels, per_device(): pl.pallas_call(functools.partial(later_exchange, group_total, coup_total)...  32.3 us
    pallas_call x2, Pallas kernels, per_device(): pl.pallas_call(functools.partial(reduce_partials, coup_total, chunks), ou...  28.2 us
    pallas_call x2, Pallas kernels, per_device(): pl.pallas_call(functools.partial(couple, coup_total, batch), out_shape=ja...  15.5 us

profile of v2, /device:TPU:15, one launch (start us, length us, event | category | flops | bytes accessed | tf_op | source)
XLA Modules:
  0.0 133.7 jit_solution(4490901476787297177)
XLA Ops:
  0.0 0.0 copy-start.1
  0.7 0.8 slice_bitcast_fusion.1
  1.5 0.8 select_reduce_fusion
  2.3 0.1 select_reduce_fusion.2
  2.4 0.1 broadcast_in_dim.50.ask_ref
  2.5 1.3 fusion.1.amp_ref
  3.8 0.0 copy-start
  3.8 1.5 %copy-done = bf16[4,448,448]{2,1,0:T(8,128)(2,1)S(1)} copy-done((bf16[4,448,448]{2,1,0:T(8,128)(2,1)S(1)}, bf16[4,448,448]{2,1,0:T(8,128)(2,1)}, u32[]{:S(2)}) %copy-start) | copy-done | bytes 1605656
  5.3 50.9 %first_exchange.1 = (bf16[8,112,448]{2,1,0:T(8,128)(2,1)S(1)}, bf16[16,448,448]{2,1,0:T(8,128)(2,1)}, s32[8,8,128]{2,1,0:T(8,128)S(1)}) custom-call(bf16[1,448,448]{2,1,0:T(8,128)(2,1)S(1)} %fusion.1.amp_ref, s32[8,8,128]{2,1,0:T(8,128)S(1)} %broadcast_in_dim.50.ask_ref, bf16[4,448,448]{2,1,0:T(8,128)(2,1)S(1)} %copy-done), custom_call_target="tpu_custom_call" | custom-call | tf_op jit(solution)/shard_map/first_exchange/pallas_call | solution.py:272
  56.2 0.0 copy-done.1
  56.2 7.8 %couple.2 = bf16[4,448,448]{2,1,0:T(8,128)(2,1)S(1)} custom-call(s32[16]{0:T(128)S(1)} %get-tuple-element.14.x_index, s32[16]{0:T(128)S(1)} %get-tuple-element.17.source, s32[16]{0:T(128)S(1)} %get-tuple-element.18.owner, s32[1]{0:T(128)} %bitcast.3.member, f32[16]{0:T(128)S(1)} %copy-done.1, bf16[8,112,448]{2,1,0:T(8,128)(2,1)S(1)} %get-tuple-element.8.amp_ref, ...), custom_call_target="tpu_custom_call" | custom-call | tf_op jit(solution)/shard_map/couple/pallas_call | solution.py:306
  64.0 0.0 copy-start.2
  64.0 0.0 copy-start.3
  64.0 13.9 %reduce_partials.2 = f32[1,448,448]{2,1,0:T(8,128)S(1)} custom-call(bf16[4,1,448,448]{3,2,1,0:T(8,128)(2,1)S(1)} %bitcast.15), custom_call_target="tpu_custom_call" | custom-call | tf_op jit(solution)/shard_map/reduce_partials/pallas_call | solution.py:329
  78.0 0.0 copy-done.2
  78.0 0.0 copy-done.3
  78.0 0.3 fusion.4.amp_ref
  78.3 32.3 %later_exchange.1.amp_ref = bf16[8,112,448]{2,1,0:T(8,128)(2,1)S(1)} custom-call(bf16[1,448,448]{2,1,0:T(8,128)(2,1)S(1)} %fusion.4.amp_ref, s32[8,8,128]{2,1,0:T(8,128)S(1)} %get-tuple-element.10.wanted), custom_call_target="tpu_custom_call" | custom-call | tf_op jit(solution)/shard_map/later_exchange/pallas_call | solution.py:294
  110.5 7.8 %couple.3 = bf16[4,448,448]{2,1,0:T(8,128)(2,1)S(1)} custom-call(s32[16]{0:T(128)S(1)} %get-tuple-element.14.x_index, s32[16]{0:T(128)S(1)} %get-tuple-element.17.source, s32[16]{0:T(128)S(1)} %get-tuple-element.18.owner, s32[1]{0:T(128)} %bitcast.3.member, f32[16]{0:T(128)S(1)} %copy-done.1, bf16[8,112,448]{2,1,0:T(8,128)(2,1)S(1)} %later_exchange.1.amp_ref, ...), custom_call_target="tpu_custom_call" | custom-call | tf_op jit(solution)/shard_map/couple/pallas_call | solution.py:306
  118.3 14.3 %reduce_partials.3 = f32[1,448,448]{2,1,0:T(8,128)S(1)} custom-call(bf16[4,1,448,448]{3,2,1,0:T(8,128)(2,1)S(1)} %bitcast.14), custom_call_target="tpu_custom_call" | custom-call | tf_op jit(solution)/shard_map/reduce_partials/pallas_call | solution.py:329
  132.6 1.2 fusion.6
  (1 shorter events, 0.0 us)
Async XLA Ops:
  0.0 56.2 %copy-start.1 = (f32[16]{0:T(128)S(1)}, f32[16]{0:T(128)}, u32[]{:S(2)}) copy-start(f32[16]{0:T(128)} %weight.3) | copy-start | bytes 196
  3.8 1.5 %copy-start = (bf16[4,448,448]{2,1,0:T(8,128)(2,1)S(1)}, bf16[4,448,448]{2,1,0:T(8,128)(2,1)}, u32[]{:S(2)}) copy-start(bf16[4,448,448]{2,1,0:T(8,128)(2,1)} %x_ref.1) | copy-start | bytes 4816900
  64.0 14.0 %copy-start.2 = (bf16[1,448,448]{2,1,0:T(8,128)(2,1)S(1)}, bf16[1,448,448]{2,1,0:T(8,128)(2,1)}, u32[]{:S(2)}) copy-start(bf16[1,448,448]{2,1,0:T(8,128)(2,1)} %param.10) | copy-start | bytes 1204228
  64.0 13.9 %copy-start.3 = (f32[1,448]{1,0:T(1,128)S(1)}, f32[1,448]{1,0:T(1,128)}, u32[]{:S(2)}) copy-start(f32[1,448]{1,0:T(1,128)} %param.11) | copy-start | bytes 5380

commit v3 on v2

--- a/solution.py
+++ b/solution.py
@@ -68,9 +68,10 @@
 
 
 def first_exchange(
-    group_total, coup_total, amp_ref, ask_ref, x_ref, arrived, x_all, asked, strips, outbuf, wanted,
+    group_total, coup_total, amp_ref, ask_ref, x_ref, tail_ref, arrived, x_all, asked, strips, outbuf, wanted,
+    packed, packed_in, unpacked,
     strip_send, strip_recv, ask_send, ask_recv, pick_send, pick_recv,
-    far_send, far_recv, sib_send, sib_recv, fwd_send, fwd_recv, local_sem, want_sem,
+    far_send, far_recv, sib_send, sib_recv, fwd_send, fwd_recv, local_sem, want_sem, put_sem,
 ):
     g, m = lax.axis_index("pairs"), lax.axis_index("coup")
     ov_dev = x_ref.shape[0]
@@ -89,19 +90,37 @@
             ask_ref.at[h], asked.at[g], ask_send.at[d], ask_recv.at[d], {"pairs": h}
         ))
     asked[g] = ask_ref[g]
+    half = x_ref.shape[1] // 2
+    main = x_all.shape[2] - tail_ref.shape[2]
+    narrow = x_ref.shape[2] - main
+    low, high = pl.ds(0, main), pl.ds(main, tail_ref.shape[2])
+    mine = pl.ds(m * ov_dev, ov_dev)
     far_copies = []
     for i in range(ov_dev):
+        packed[i] = jnp.concatenate(
+            [tail_ref[i, :half, :narrow], tail_ref[i, half:, :narrow]], axis=-1
+        )
         for d in range(1, chips):
-            peer = lax.rem(chip + d, chips) * 2 + core
+            peer = {"coup": lax.rem(chip + d, chips) * 2 + core}
             far_copies.append((d, i, remote(
-                x_ref.at[i], x_all.at[m * ov_dev + i],
-                far_send.at[d, i], far_recv.at[d, i], {"coup": peer},
+                x_ref.at[i, :, low], x_all.at[m * ov_dev + i, :, low],
+                far_send.at[0, d, i], far_recv.at[0, d, i], peer,
+            ), remote(
+                packed.at[i], packed_in.at[d, i],
+                far_send.at[1, d, i], far_recv.at[1, d, i], peer,
             )))
-    sib_copy = remote(
-        x_ref, x_all.at[pl.ds(m * ov_dev, ov_dev)], sib_send, sib_recv, {"coup": sibling}
-    )
-    own_copy = pltpu.make_async_copy(x_ref, x_all.at[pl.ds(m * ov_dev, ov_dev)], local_sem)
-    own_copy.start()
+    near_copies = [
+        remote(x_ref.at[:, :, low], x_all.at[mine, :, low],
+               sib_send.at[0], sib_recv.at[0], {"coup": sibling}),
+        remote(tail_ref, x_all.at[mine, :, high],
+               sib_send.at[1], sib_recv.at[1], {"coup": sibling}),
+    ]
+    own_copies = [
+        pltpu.make_async_copy(x_ref.at[:, :, low], x_all.at[mine, :, low], local_sem.at[0]),
+        pltpu.make_async_copy(tail_ref, x_all.at[mine, :, high], local_sem.at[1]),
+    ]
+    for copy in own_copies:
+        copy.start()
     for copy in ask_copies:
         copy.wait_recv()
     want_copy = pltpu.make_async_copy(asked, wanted, want_sem)
@@ -113,18 +132,29 @@
         wanted, strips, outbuf, arrived, pick_send, pick_recv, g, group_total
     )
     forwards = []
-    for d, i, copy in far_copies:
-        copy.wait_recv()
+    for d, i, main_copy, tail_copy in far_copies:
         origin = lax.rem(chip - d + chips, chips) * 2 + core
-        slot = x_all.at[origin * ov_dev + i]
+        slot = origin * ov_dev + i
+        main_copy.wait_recv()
+        there = x_all.at[slot, :, low]
         forwards.append(remote(
-            slot, slot, fwd_send.at[d, i], fwd_recv.at[d, i], {"coup": sibling}
+            there, there, fwd_send.at[0, d, i], fwd_recv.at[0, d, i], {"coup": sibling}
         ))
-    own_copy.wait()
-    sib_copy.wait()
-    for copy in forwards + pick_copies:
+        tail_copy.wait_recv()
+        block = packed_in[d, i]
+        unpacked[d, i, :half] = block
+        unpacked[d, i, half:] = jnp.concatenate([block[:, narrow:], block[:, :narrow]], axis=-1)
+        there = x_all.at[slot, :, high]
+        forwards.append(remote(
+            unpacked.at[d, i], there, fwd_send.at[1, d, i], fwd_recv.at[1, d, i],
+            {"coup": sibling},
+        ))
+        put = pltpu.make_async_copy(unpacked.at[d, i], there, put_sem.at[d, i])
+        put.start()
+        own_copies.append(put)
+    for copy in own_copies + near_copies + forwards + pick_copies:
         copy.wait()
-    for copy in strip_copies + ask_copies + [c for _, _, c in far_copies]:
+    for copy in strip_copies + ask_copies + [c for far in far_copies for c in far[2:]]:
         copy.wait_send()
 
 
@@ -204,7 +234,7 @@
         last = min(pl.cdiv(low + rows, 128) * 128, width)
         for b in range(batch):
             right = lax.dot_general(
-                amp_ref[source[k * batch + b]], x_refs[b][0],
+                amp_ref[source[k * batch + b]], x_refs[b][0, :, :width],
                 (((1,), (1,)), ((), ())), preferred_element_type=jnp.float32,
             )
             padded[b, low:low + rows] = (right * weight[k * batch + b]).astype(jnp.bfloat16)
@@ -256,6 +286,9 @@
     integral_f = integrals.astype(jnp.float32)
     rounded = (-integral_f / denominator).astype(jnp.bfloat16)
 
+    wide = pl.cdiv(width, 128) * 128
+    tails = jnp.pad(intersections[:, :, wide - 128:], ((0, 0), (0, 0), (0, wide - width)))
+
     vmem = pl.BlockSpec(memory_space=pltpu.VMEM)
     smem = pl.BlockSpec(memory_space=pltpu.SMEM)
     anywhere = pl.BlockSpec(memory_space=pl.ANY)
@@ -273,21 +306,25 @@
         functools.partial(first_exchange, group_total, coup_total),
         out_shape=(
             arrived_shape,
-            jax.ShapeDtypeStruct((ov_dev * coup_total, width, width), jnp.bfloat16),
+            jax.ShapeDtypeStruct((ov_dev * coup_total, width, wide), jnp.bfloat16),
             jax.ShapeDtypeStruct((group_total, 8, 128), jnp.int32),
         ),
-        in_specs=[vmem, vmem, anywhere],
+        in_specs=[vmem, vmem, anywhere, vmem],
         out_specs=(vmem, anywhere, vmem),
         scratch_shapes=[
             strips_scratch, out_scratch, pltpu.SMEM((group_total, 8, 128), jnp.int32),
+            pltpu.VMEM((ov_dev, width // 2, 128), jnp.bfloat16),
+            pltpu.VMEM((chips, ov_dev, width // 2, 128), jnp.bfloat16),
+            pltpu.VMEM((chips, ov_dev, width, 128), jnp.bfloat16),
             dma((coup_total,)), dma((coup_total,)), dma((group_total,)), dma((group_total,)),
             dma((group_total,)), dma((group_total,)),
-            dma((chips, ov_dev)), dma((chips, ov_dev)), dma, dma,
-            dma((chips, ov_dev)), dma((chips, ov_dev)), dma, dma,
+            dma((2, chips, ov_dev)), dma((2, chips, ov_dev)), dma((2,)), dma((2,)),
+            dma((2, chips, ov_dev)), dma((2, chips, ov_dev)), dma((2,)), dma,
+            dma((chips, ov_dev)),
         ],
         compiler_params=params(0),
         name="first_exchange",
-    )(rounded, ask, intersections)
+    )(rounded, ask, intersections, tails)
 
     for iteration in range(ITERS):
         if iteration > 0:
@@ -313,7 +350,7 @@
                     smem,
                     pl.BlockSpec((group_total, rows, width), lambda k, *_: (0, 0, 0)),
                 ] + [
-                    pl.BlockSpec((1, width, width), lambda k, xi, *_, b=b: (xi[k * batch + b], 0, 0))
+                    pl.BlockSpec((1, width, wide), lambda k, xi, *_, b=b: (xi[k * batch + b], 0, 0))
                     for b in range(batch)
                 ],
                 out_specs=pl.BlockSpec((group_pairs, width, width), lambda k, *_: (0, 0, 0)),

time: 134 us -> 127 us (0.948)
  Pallas kernels: 127 us -> 122 us
  local copies, waits for them, and re-layouts: 1.59 us -> 0.19 us
    pallas_call x1, Pallas kernels: 50.9 us -> 45.7 us  [per_device(): pl.pallas_call(functools.partial(first_exchange, group_total, coup_total)...]
    unnamed x8, local copies, waits for them, and re-layouts: 1.51 us -> 0.02 us
where the time goes in v3:
time: 127 us
  Pallas kernels  122 us (96%)
  other arithmetic  4.48 us (4%)
    pallas_call x1, Pallas kernels, per_device(): pl.pallas_call(functools.partial(first_exchange, group_total, coup_total)...  45.7 us
    pallas_call x1, Pallas kernels, per_device(): pl.pallas_call(functools.partial(later_exchange, group_total, coup_total)...  31.6 us
    pallas_call x2, Pallas kernels, per_device(): pl.pallas_call(functools.partial(reduce_partials, coup_total, chunks), ou...  28.2 us
    pallas_call x2, Pallas kernels, per_device(): pl.pallas_call(functools.partial(couple, coup_total, batch), out_shape=ja...  16 us

profile of v3, /device:TPU:15, one launch (start us, length us, event | category | flops | bytes accessed | tf_op | source)
XLA Modules:
  0.0 127.2 jit_solution(15665985880609394972)
XLA Ops:
  0.0 0.0 slice-start
  0.0 0.0 copy-start
  0.8 0.8 slice_bitcast_fusion.1
  1.6 0.8 select_reduce_fusion
  2.5 0.1 select_reduce_fusion.2
  2.6 0.1 broadcast_in_dim.50.ask_ref
  2.7 1.3 %fusion.1.amp_ref = bf16[1,448,448]{2,1,0:T(8,128)(2,1)S(1)} fusion(bf16[1,448,448]{2,1,0:T(8,128)(2,1)} %param.10, f32[]{:T(128)} %bitcast.11, f32[448]{0:T(512)} %bitcast.16), kind=kLoop, calls=%fused_computation.4 | loop fusion | flops 1204224 | bytes 804612 | tf_op jit(solution)/shard_map/convert_element_type | solution.py:287
  3.9 0.0 slice-done
  3.9 0.0 copy-start.1
  4.0 0.1 pad.4.tail_ref
  4.1 0.0 copy-done
  4.1 45.7 %first_exchange.1 = (bf16[8,112,448]{2,1,0:T(8,128)(2,1)S(1)}, bf16[16,448,512]{2,1,0:T(8,128)(2,1)}, s32[8,8,128]{2,1,0:T(8,128)S(1)}) custom-call(bf16[1,448,448]{2,1,0:T(8,128)(2,1)S(1)} %fusion.1.amp_ref, s32[8,8,128]{2,1,0:T(8,128)S(1)} %broadcast_in_dim.50.ask_ref, bf16[4,448,448]{2,1,0:T(8,128)(2,1)S(1)} %copy-done, bf16[4,448,128]{2,1,0:T(8,128)(2,1)S(1)} %pad.4.tail_ref), custom_call_target="tpu_custom_call" | custom-call | tf_op jit(solution)/shard_map/first_exchange/pallas_call | solution.py:305
  49.8 0.0 copy-done.1
  49.8 8.0 %couple.2 = bf16[4,448,448]{2,1,0:T(8,128)(2,1)S(1)} custom-call(s32[16]{0:T(128)S(1)} %get-tuple-element.14.x_index, s32[16]{0:T(128)S(1)} %get-tuple-element.17.source, s32[16]{0:T(128)S(1)} %get-tuple-element.18.owner, s32[1]{0:T(128)} %bitcast.3.member, f32[16]{0:T(128)S(1)} %copy-done.1, bf16[8,112,448]{2,1,0:T(8,128)(2,1)S(1)} %get-tuple-element.8.amp_ref, ...), custom_call_target="tpu_custom_call" | custom-call | tf_op jit(solution)/shard_map/couple/pallas_call | solution.py:343
  57.8 0.0 copy-start.2
  57.9 0.0 copy-start.3
  57.9 14.0 %reduce_partials.2 = f32[1,448,448]{2,1,0:T(8,128)S(1)} custom-call(bf16[4,1,448,448]{3,2,1,0:T(8,128)(2,1)S(1)} %bitcast.15), custom_call_target="tpu_custom_call" | custom-call | tf_op jit(solution)/shard_map/reduce_partials/pallas_call | solution.py:366
  71.8 0.0 copy-done.2
  71.8 0.0 copy-done.3
  71.9 0.3 fusion.4.amp_ref
  72.1 31.6 %later_exchange.1.amp_ref = bf16[8,112,448]{2,1,0:T(8,128)(2,1)S(1)} custom-call(bf16[1,448,448]{2,1,0:T(8,128)(2,1)S(1)} %fusion.4.amp_ref, s32[8,8,128]{2,1,0:T(8,128)S(1)} %get-tuple-element.10.wanted), custom_call_target="tpu_custom_call" | custom-call | tf_op jit(solution)/shard_map/later_exchange/pallas_call | solution.py:331
  103.8 8.0 %couple.3 = bf16[4,448,448]{2,1,0:T(8,128)(2,1)S(1)} custom-call(s32[16]{0:T(128)S(1)} %get-tuple-element.14.x_index, s32[16]{0:T(128)S(1)} %get-tuple-element.17.source, s32[16]{0:T(128)S(1)} %get-tuple-element.18.owner, s32[1]{0:T(128)} %bitcast.3.member, f32[16]{0:T(128)S(1)} %copy-done.1, bf16[8,112,448]{2,1,0:T(8,128)(2,1)S(1)} %later_exchange.1.amp_ref, ...), custom_call_target="tpu_custom_call" | custom-call | tf_op jit(solution)/shard_map/couple/pallas_call | solution.py:343
  111.8 14.2 %reduce_partials.3 = f32[1,448,448]{2,1,0:T(8,128)S(1)} custom-call(bf16[4,1,448,448]{3,2,1,0:T(8,128)(2,1)S(1)} %bitcast.14), custom_call_target="tpu_custom_call" | custom-call | tf_op jit(solution)/shard_map/reduce_partials/pallas_call | solution.py:366
  126.0 1.2 fusion.6
  (1 shorter events, 0.0 us)
Async XLA Ops:
  0.0 3.9 %slice-start = ((bf16[4,448,448]{2,1,0:T(8,128)(2,1)}), bf16[4,448,64]{2,1,0:T(8,128)(2,1)S(1)}, s32[]{:S(2)}) async-start(bf16[4,448,448]{2,1,0:T(8,128)(2,1)} %x_ref.1), calls=%async_computation | async-start | bytes 917504 | tf_op jit(solution)/shard_map/slice | solution.py:290
  0.0 4.1 %copy-start = (bf16[4,448,448]{2,1,0:T(8,128)(2,1)S(1)}, bf16[4,448,448]{2,1,0:T(8,128)(2,1)}, u32[]{:S(2)}) copy-start(bf16[4,448,448]{2,1,0:T(8,128)(2,1)} %x_ref.1) | copy-start | bytes 4816900
  3.9 45.9 %copy-start.1 = (f32[16]{0:T(128)S(1)}, f32[16]{0:T(128)}, u32[]{:S(2)}) copy-start(f32[16]{0:T(128)} %weight.3) | copy-start | bytes 196
  57.8 14.0 %copy-start.2 = (bf16[1,448,448]{2,1,0:T(8,128)(2,1)S(1)}, bf16[1,448,448]{2,1,0:T(8,128)(2,1)}, u32[]{:S(2)}) copy-start(bf16[1,448,448]{2,1,0:T(8,128)(2,1)} %param.10) | copy-start | bytes 1204228
  57.9 14.0 %copy-start.3 = (f32[1,448]{1,0:T(1,128)S(1)}, f32[1,448]{1,0:T(1,128)}, u32[]{:S(2)}) copy-start(f32[1,448]{1,0:T(1,128)} %param.11) | copy-start | bytes 5380

commit v4 on v3

--- a/solution.py
+++ b/solution.py
@@ -187,7 +187,7 @@
     chip, core = m // 2, lax.rem(m, 2)
     sibling = chip * 2 + 1 - core
     peers = [lax.rem(chip + d, chips) * 2 for d in range(chips)]
-    size = total.shape[1] // chunks
+    size = part.shape[2] // chunks
     rows = [slice(c * size, (c + 1) * size) for c in range(chunks)]
     order = [(d, c) for d in list(range(1, chips)) + [0] for c in range(chunks)]
     greet([{"coup": sibling}] + [{"coup": peers[d] + core} for d in range(1, chips)])
@@ -198,22 +198,33 @@
             near_send.at[d, c], near_recv.at[d, c], {"coup": sibling},
         )
     far_copies = []
-    for d, c in order:
+    far_copies = {}
+
+    def own_chip(d, c):
         near_copies[d, c].wait_recv()
         both = part[peers[d] + core, :, rows[c]].astype(jnp.float32)
-        both += near[d, :, rows[c]].astype(jnp.float32)
-        if d == 0:
-            total[:, rows[c]] = both
-        else:
-            joined[d, :, rows[c]] = both.astype(jnp.bfloat16)
-            far_copies.append((d, c, remote(
+        return both + near[d, :, rows[c]].astype(jnp.float32)
+
+    for d, c in order:
+        if d > 0:
+            joined[d, :, rows[c]] = own_chip(d, c).astype(jnp.bfloat16)
+            far_copies[d, c] = remote(
                 joined.at[d, :, rows[c]], far.at[d, :, rows[c]],
                 far_send.at[d, c], far_recv.at[d, c], {"coup": peers[d] + core},
-            )))
-    for d, c, copy in far_copies:
-        copy.wait_recv()
-        total[:, rows[c]] += far[d, :, rows[c]].astype(jnp.float32)
-    for _, _, copy in far_copies:
+            )
+    narrow = total.shape[2] % 128
+    for c in range(chunks):
+        value = own_chip(0, c)
+        for d in range(1, chips):
+            far_copies[d, c].wait_recv()
+            value += far[d, :, rows[c]].astype(jnp.float32)
+        left = c // 2 * 128
+        if c < chunks - 1:
+            total[:, c % 2 * size:(c % 2 + 1) * size, left:left + 128] = value
+        else:
+            total[:, :size, left:] = value[:, :, :narrow]
+            total[:, size:, left:] = value[:, :, narrow:]
+    for copy in far_copies.values():
         copy.wait_send()
     for d, c in order:
         near_copies[d, c].wait_send()
@@ -250,7 +261,14 @@
     @pl.when(k == pl.num_programs(0) - 1)
     def _():
         for p in range(acc.shape[0]):
-            out_ref[p] = acc[p].astype(jnp.bfloat16)
+            for left in range(0, width - 127, 128):
+                out_ref[p, left // 128 * width:(left // 128 + 1) * width] = (
+                    acc[p, :, left:left + 128].astype(jnp.bfloat16)
+                )
+            left = width // 128 * 128
+            out_ref[p, left // 128 * width:] = jnp.concatenate(
+                [acc[p, :width // 2, left:], acc[p, width // 2:, left:]], axis=-1
+            ).astype(jnp.bfloat16)
 
 
 def per_device(
@@ -267,7 +285,8 @@
     rows = width // coup_total
     chips = coup_total // 2
     batch = math.gcd(couplings, 4)
-    chunks = math.gcd(width // 16, 4)
+    chunks = width // 64
+    stacked = chunks * (width // 2)
 
     owner_row = lookup(pair_slot, coupling_list[0])
     reader_row = lookup(pair_slot, coupling_list[1])
@@ -342,7 +361,7 @@
             )(rounded, asked)
         part = pl.pallas_call(
             functools.partial(couple, coup_total, batch),
-            out_shape=jax.ShapeDtypeStruct((group_pairs, width, width), jnp.bfloat16),
+            out_shape=jax.ShapeDtypeStruct((group_pairs, stacked, 128), jnp.bfloat16),
             grid_spec=pltpu.PrefetchScalarGridSpec(
                 num_scalar_prefetch=4,
                 grid=(couplings // batch,),
@@ -353,7 +372,7 @@
                     pl.BlockSpec((1, width, wide), lambda k, xi, *_, b=b: (xi[k * batch + b], 0, 0))
                     for b in range(batch)
                 ],
-                out_specs=pl.BlockSpec((group_pairs, width, width), lambda k, *_: (0, 0, 0)),
+                out_specs=pl.BlockSpec((group_pairs, stacked, 128), lambda k, *_: (0, 0, 0)),
                 scratch_shapes=[
                     pltpu.VMEM((group_pairs, width, width), jnp.float32),
                     pltpu.VMEM((batch, width, width), jnp.bfloat16),
@@ -363,20 +382,21 @@
             name="couple",
         )(x_index, source, owner, member[None], coupling_weight, arrived, *[x_all] * batch)
         block = (pair_dev, width, width)
+        packed_block = (pair_dev, stacked, 128)
         coupled = pl.pallas_call(
             functools.partial(reduce_partials, coup_total, chunks),
             out_shape=jax.ShapeDtypeStruct(block, jnp.float32),
             in_specs=[vmem],
             out_specs=vmem,
             scratch_shapes=[
-                pltpu.VMEM((chips,) + block, jnp.bfloat16),
-                pltpu.VMEM((chips,) + block, jnp.bfloat16),
-                pltpu.VMEM((chips,) + block, jnp.bfloat16),
+                pltpu.VMEM((chips,) + packed_block, jnp.bfloat16),
+                pltpu.VMEM((chips,) + packed_block, jnp.bfloat16),
+                pltpu.VMEM((chips,) + packed_block, jnp.bfloat16),
                 *[dma((chips, chunks))] * 4,
             ],
             compiler_params=params(2),
             name="reduce_partials",
-        )(part.reshape((coup_total,) + block))
+        )(part.reshape((coup_total,) + packed_block))
         amplitudes = -(integral_f + coupled) / denominator
         rounded = amplitudes.astype(jnp.bfloat16)
     return amplitudes

time: 127 us -> 126 us (level)
  Pallas kernels: 122 us -> 120 us
    pallas_call x2, Pallas kernels: 28.2 us -> 26.2 us  [per_device(): pl.pallas_call(functools.partial(reduce_partials, coup_total, chunks), ou...]
where the time goes in v4:
time: 126 us; the launch traced here: 125 us
  Pallas kernels  120 us (95%)
  other arithmetic  4.48 us (4%)
    pallas_call x1, Pallas kernels, per_device(): pl.pallas_call(functools.partial(first_exchange, group_total, coup_total)...  45.7 us
    pallas_call x1, Pallas kernels, per_device(): pl.pallas_call(functools.partial(later_exchange, group_total, coup_total)...  32.2 us
    pallas_call x2, Pallas kernels, per_device(): pl.pallas_call(functools.partial(reduce_partials, coup_total, chunks), ou...  26.2 us
    pallas_call x2, Pallas kernels, per_device(): pl.pallas_call(functools.partial(couple, coup_total, batch), out_shape=ja...  15.7 us

profile of v4, /device:TPU:15, one launch (start us, length us, event | category | flops | bytes accessed | tf_op | source)
XLA Modules:
  0.0 125.3 jit_solution(4045685989236361161)
XLA Ops:
  0.0 0.0 slice-start
  0.0 0.0 copy-start
  0.8 0.8 slice_bitcast_fusion.1
  1.6 0.8 select_reduce_fusion
  2.5 0.1 select_reduce_fusion.2
  2.6 0.1 broadcast_in_dim.50.ask_ref
  2.7 1.3 %fusion.1.amp_ref = bf16[1,448,448]{2,1,0:T(8,128)(2,1)S(1)} fusion(bf16[1,448,448]{2,1,0:T(8,128)(2,1)} %param.10, f32[]{:T(128)} %bitcast.11, f32[448]{0:T(512)} %bitcast.16), kind=kLoop, calls=%fused_computation.4 | loop fusion | flops 1204224 | bytes 804612 | tf_op jit(solution)/shard_map/convert_element_type | solution.py:306
  3.9 0.0 slice-done
  3.9 0.0 copy-start.1
  4.0 0.1 pad.4.tail_ref
  4.1 0.0 copy-done
  4.1 45.7 %first_exchange.1 = (bf16[8,112,448]{2,1,0:T(8,128)(2,1)S(1)}, bf16[16,448,512]{2,1,0:T(8,128)(2,1)}, s32[8,8,128]{2,1,0:T(8,128)S(1)}) custom-call(bf16[1,448,448]{2,1,0:T(8,128)(2,1)S(1)} %fusion.1.amp_ref, s32[8,8,128]{2,1,0:T(8,128)S(1)} %broadcast_in_dim.50.ask_ref, bf16[4,448,448]{2,1,0:T(8,128)(2,1)S(1)} %copy-done, bf16[4,448,128]{2,1,0:T(8,128)(2,1)S(1)} %pad.4.tail_ref), custom_call_target="tpu_custom_call" | custom-call | tf_op jit(solution)/shard_map/first_exchange/pallas_call | solution.py:324
  49.8 0.0 copy-done.1
  49.8 7.8 %couple.2 = bf16[4,1568,128]{2,1,0:T(8,128)(2,1)S(1)} custom-call(s32[16]{0:T(128)S(1)} %get-tuple-element.14.x_index, s32[16]{0:T(128)S(1)} %get-tuple-element.17.source, s32[16]{0:T(128)S(1)} %get-tuple-element.18.owner, s32[1]{0:T(128)} %bitcast.3.member, f32[16]{0:T(128)S(1)} %copy-done.1, bf16[8,112,448]{2,1,0:T(8,128)(2,1)S(1)} %get-tuple-element.8.amp_ref, ...), custom_call_target="tpu_custom_call" | custom-call | tf_op jit(solution)/shard_map/couple/pallas_call | solution.py:362
  57.7 0.0 copy-start.2
  57.7 0.0 copy-start.3
  57.7 12.9 %reduce_partials.2 = f32[1,448,448]{2,1,0:T(8,128)S(1)} custom-call(bf16[4,1,1568,128]{3,2,1,0:T(8,128)(2,1)S(1)} %bitcast.15), custom_call_target="tpu_custom_call" | custom-call | tf_op jit(solution)/shard_map/reduce_partials/pallas_call | solution.py:386
  70.6 0.0 copy-done.2
  70.6 0.0 copy-done.3
  70.6 0.3 fusion.4.amp_ref
  70.9 32.2 %later_exchange.1.amp_ref = bf16[8,112,448]{2,1,0:T(8,128)(2,1)S(1)} custom-call(bf16[1,448,448]{2,1,0:T(8,128)(2,1)S(1)} %fusion.4.amp_ref, s32[8,8,128]{2,1,0:T(8,128)S(1)} %get-tuple-element.10.wanted), custom_call_target="tpu_custom_call" | custom-call | tf_op jit(solution)/shard_map/later_exchange/pallas_call | solution.py:350
  103.1 7.8 %couple.3 = bf16[4,1568,128]{2,1,0:T(8,128)(2,1)S(1)} custom-call(s32[16]{0:T(128)S(1)} %get-tuple-element.14.x_index, s32[16]{0:T(128)S(1)} %get-tuple-element.17.source, s32[16]{0:T(128)S(1)} %get-tuple-element.18.owner, s32[1]{0:T(128)} %bitcast.3.member, f32[16]{0:T(128)S(1)} %copy-done.1, bf16[8,112,448]{2,1,0:T(8,128)(2,1)S(1)} %later_exchange.1.amp_ref, ...), custom_call_target="tpu_custom_call" | custom-call | tf_op jit(solution)/shard_map/couple/pallas_call | solution.py:362
  110.9 13.2 %reduce_partials.3 = f32[1,448,448]{2,1,0:T(8,128)S(1)} custom-call(bf16[4,1,1568,128]{3,2,1,0:T(8,128)(2,1)S(1)} %bitcast.14), custom_call_target="tpu_custom_call" | custom-call | tf_op jit(solution)/shard_map/reduce_partials/pallas_call | solution.py:386
  124.2 1.2 fusion.6
  (1 shorter events, 0.0 us)
Async XLA Ops:
  0.0 3.9 %slice-start = ((bf16[4,448,448]{2,1,0:T(8,128)(2,1)}), bf16[4,448,64]{2,1,0:T(8,128)(2,1)S(1)}, s32[]{:S(2)}) async-start(bf16[4,448,448]{2,1,0:T(8,128)(2,1)} %x_ref.1), calls=%async_computation | async-start | bytes 917504 | tf_op jit(solution)/shard_map/slice | solution.py:309
  0.0 4.1 %copy-start = (bf16[4,448,448]{2,1,0:T(8,128)(2,1)S(1)}, bf16[4,448,448]{2,1,0:T(8,128)(2,1)}, u32[]{:S(2)}) copy-start(bf16[4,448,448]{2,1,0:T(8,128)(2,1)} %x_ref.1) | copy-start | bytes 4816900
  3.9 45.9 %copy-start.1 = (f32[16]{0:T(128)S(1)}, f32[16]{0:T(128)}, u32[]{:S(2)}) copy-start(f32[16]{0:T(128)} %weight.3) | copy-start | bytes 196
  57.7 13.0 %copy-start.2 = (bf16[1,448,448]{2,1,0:T(8,128)(2,1)S(1)}, bf16[1,448,448]{2,1,0:T(8,128)(2,1)}, u32[]{:S(2)}) copy-start(bf16[1,448,448]{2,1,0:T(8,128)(2,1)} %param.10) | copy-start | bytes 1204228
  57.7 12.9 %copy-start.3 = (f32[1,448]{1,0:T(1,128)S(1)}, f32[1,448]{1,0:T(1,128)}, u32[]{:S(2)}) copy-start(f32[1,448]{1,0:T(1,128)} %param.11) | copy-start | bytes 5380
